TPU v7x, 32 devices: a whole 2x2x4 slice. The times are simulated.
32 devices in a mesh: lon: 8 (over y, x, core), lat: 4 (over z).
Axes of the slice: x: 2, y: 2, z: 4, core: 2. Of those that a mesh axis runs over, the one named last changes fastest.
Arguments:
- ocean_state: float32 [4, 8, 2048, 512], P(None, None, 'lon', 'lat'), may hold values from -6 to 6
- diffusivity: float32 [7, 2048, 512], P(None, 'lon', 'lat'), may hold values from 0.05 to 2
- land_mask: int32 [2048, 512], P('lon', 'lat'), may hold values from 0 to 1, as said below
- tile_plan: int32 [16, 4], P(None, 'lat'), may hold values from 0 to 15, as said below
Outputs:
- moved_state: float32 [4, 8, 2048, 512], P(None, None, 'lon', 'lat')
Inputs may be any that keep to these rules, and one draw needn't show every extreme that they name: `land_mask`: tiles of 128 x 128 columns may be land throughout; others are ocean throughout or mixed. Each column of tile_plan is a permutation of 0 to 15; a tile whose columns are all land keeps its position; every tile lands within 3 tile positions of where it stands, counted around the longitude loop; in some row one tile moves 3 positions east and one 3 positions west.
All inputs are finite; a program needn't handle non-finite values.
Results may differ from a plain program's by a relative error of at most 0.00002.
Values sent between devices are 32-bit elements; how exact they have to be, the bound alone decides.
A program may use at most 128 MiB of HBM per device.

v0:
```python
import functools

import jax
import jax.numpy as jnp
from jax import lax
from jax.experimental import pallas as pl
from jax.experimental.pallas import tpu as pltpu
from jax.sharding import PartitionSpec as P

advect_coef = 0.1
diffuse_coef = 0.1
gradient_coef = 0.1
thermal_coef = 0.2
haline_coef = 0.15
weight_coef = 0.25

F32 = jnp.float32
MIB = 1 << 20
MESH = pl.DeviceIdType.MESH
STEP = 8
RELAYED = ((1, 4), (2,))


def remote_copy(source, target, send, recv, who):
    return pltpu.make_async_remote_copy(
        src_ref=source, dst_ref=target, send_sem=send, recv_sem=recv, device_id=who, device_id_type=MESH
    )


def halo_kernel(
    relays,
    plan_ref,
    state_ref,
    mask_ref,
    lat_ref,
    west_ref,
    east_ref,
    branch_ref,
    held,
    mask,
    lat_pack,
    lon_pack,
    north_in,
    south_in,
    west_in,
    east_in,
    count,
    counts_in,
    load_sem,
    send_sem,
    recv_sem,
):
    fields, levels, rows, lanes = held.shape
    half = rows // 2
    lane = lax.broadcasted_iota(jnp.int32, (8, lanes), 1)
    devices, bands = lax.axis_size("lon"), lax.axis_size("lat")
    lon, lat = lax.axis_index("lon"), lax.axis_index("lat")
    top = lat == bands - 1
    to_east = {"lon": lax.rem(lon + 1, devices)}
    to_west = {"lon": lax.rem(lon + devices - 1, devices)}
    across = {"lon": devices - 1 - lon}
    others = [{"lat": lax.rem(lat + o, bands)} for o in range(1, bands)]
    barrier = pltpu.get_barrier_semaphore()
    for who in [to_east, to_west, across] + others:
        pl.semaphore_signal(barrier, inc=1, device_id=who, device_id_type=MESH)

    mask_load = pltpu.make_async_copy(mask_ref, mask, load_sem.at[fields])
    mask_load.start()
    loads = [pltpu.make_async_copy(state_ref.at[f], held.at[f], load_sem.at[f]) for f in range(fields)]
    for load in loads:
        load.start()

    chips = devices // 2

    def leaving(chip, most):
        for way in (1, -1):
            number = jnp.int32(0)
            for t in range(4):
                number = number + leaves(plan_ref, chips, chip, t, way).astype(jnp.int32)
            most = jnp.maximum(most, number)
        return most

    most = lax.fori_loop(0, chips, leaving, jnp.int32(0))
    count[...] = jnp.full(count.shape, most, jnp.int32)
    mask_load.wait()
    first = mask[0:1, :].astype(F32)
    final = mask[rows - 1 : rows, :].astype(F32)
    for f in range(fields):
        loads[f].wait()

        def group(g, _):
            to = pl.ds(pl.multiple_of(g * 8, 8), 8)
            part = lat_pack[to, :] if f > 0 else jnp.zeros((8, lanes), F32)
            for slot in range(2):
                at = pl.ds(pl.multiple_of(slot * half + g * 8, 8), 8)
                wet = mask[at, :].astype(F32)
                for k in range(levels):
                    place = 64 * slot + 2 * (f * levels + k)
                    x = pltpu.roll(held[f, k, at, :] * wet, place + 1, 1)
                    part = jnp.where((lane >> 1) == (place >> 1), x, part)
            lat_pack[to, :] = part
            return 0

        lax.fori_loop(0, half // 8, group, 0, unroll=2)
        at_field = slice(f * levels, (f + 1) * levels)
        lon_pack[0, at_field, :] = jnp.concatenate([held[f, k, 0:1, :] for k in range(levels)], 0) * first
        lon_pack[1, at_field, :] = (
            jnp.concatenate([held[f, k, rows - 1 : rows, :] for k in range(levels)], 0) * final
        )

    pl.semaphore_wait(barrier, 3 + bands - 1)

    def remote(source, target, at, recv_at, who):
        return remote_copy(source, target, send_sem.at[at], recv_sem.at[recv_at], who)

    up = remote(lat_pack, south_in, 0, 0, {"lat": jnp.minimum(lat + 1, bands - 1)})
    down = remote(lat_pack, north_in, 1, 1, {"lat": jnp.maximum(lat - 1, 0)})
    fold = remote(lat_pack, north_in, 0, 1, across)
    east = remote(lon_pack.at[1], west_in, 2, 2, to_east)
    west = remote(lon_pack.at[0], east_in, 3, 3, to_west)
    tell = [remote(count, counts_in.at[o], 4 + o, 4 + o, who) for o, who in enumerate(others)]
    pl.when(top)(fold.start)
    pl.when(jnp.logical_not(top))(up.start)
    pl.when(lat > 0)(down.start)
    for t in tell:
        t.start()
    east.start()
    west.start()

    values = [count[...]]
    value_rows = [lat]
    for o, t in enumerate(tell):
        t.wait_recv()
        values.append(counts_in[o])
        value_rows.append(lax.rem(lat + bands - o - 1, bands))
    largest, idle = values[0], jnp.full(count.shape, bands, jnp.int32)
    for value, row in zip(values, value_rows):
        largest = jnp.maximum(largest, value)
        idle = jnp.minimum(idle, jnp.where(value == 0, row, bands))
    if relays:
        branch = jnp.where(largest <= 1, idle, bands - 1 + largest)
    else:
        branch = jnp.maximum(largest, 1) - 1
    branch_ref[0] = jnp.max(branch)
    east.wait_recv()
    west_ref[...] = west_in[...]
    west.wait_recv()
    east_ref[...] = east_in[...]

    @pl.when(lat > 0)
    def _():
        up.wait_recv()

    @pl.when(lat == 0)
    def _():
        south_in[...] = jnp.zeros_like(south_in)

    down.wait_recv()
    place = lax.broadcasted_iota(jnp.int32, (half, lanes), 1)
    south = pltpu.roll(south_in[...], 2, 1)

    @pl.when(top)
    def _():
        r = lax.broadcasted_iota(jnp.int32, (half, half), 0)
        c = lax.broadcasted_iota(jnp.int32, (half, half), 1)
        turn = jnp.where(r + c == half - 1, 1.0, 0.0).astype(F32)
        mirror = jnp.dot(turn, north_in[...], precision=lax.Precision.HIGHEST, preferred_element_type=F32)
        mirror = pltpu.roll(mirror, 65, 1)
        mirror = jnp.where((place & 63) >= 32, -mirror, mirror)
        lat_ref[...] = jnp.where((place & 1) == 1, mirror, south)

    @pl.when(jnp.logical_not(top))
    def _():
        lat_ref[...] = jnp.where((place & 1) == 1, north_in[...], south)

    up.wait_send()
    pl.when(lat > 0)(down.wait_send)
    east.wait_send()
    west.wait_send()
    for t in tell:
        t.wait_send()


def halos(relays, plan, state, mask):
    fields, levels, rows, lanes = state.shape
    bands = lax.axis_size("lat")
    pack = (rows // 2, lanes)
    edge = (fields * levels, lanes)
    near = pl.BlockSpec(memory_space=pltpu.VMEM)
    anywhere = pl.BlockSpec(memory_space=pl.ANY)
    scalars = pl.BlockSpec(memory_space=pltpu.SMEM)
    return pl.pallas_call(
        functools.partial(halo_kernel, relays),
        in_specs=[scalars, anywhere, anywhere],
        out_specs=[near, near, near, scalars],
        out_shape=[
            jax.ShapeDtypeStruct(pack, F32),
            jax.ShapeDtypeStruct(edge, F32),
            jax.ShapeDtypeStruct(edge, F32),
            jax.ShapeDtypeStruct((1,), jnp.int32),
        ],
        scratch_shapes=[
            pltpu.VMEM(state.shape, F32),
            pltpu.VMEM(mask.shape, jnp.int32),
            pltpu.VMEM(pack, F32),
            pltpu.VMEM((2,) + edge, F32),
            pltpu.VMEM(pack, F32),
            pltpu.VMEM(pack, F32),
            pltpu.VMEM(edge, F32),
            pltpu.VMEM(edge, F32),
            pltpu.VMEM((8, lanes), jnp.int32),
            pltpu.VMEM((bands - 1, 8, lanes), jnp.int32),
            pltpu.SemaphoreType.DMA((fields + 1,)),
            pltpu.SemaphoreType.DMA((4 + bands - 1,)),
            pltpu.SemaphoreType.DMA((4 + bands - 1,)),
        ],
        compiler_params=pltpu.CompilerParams(
            collective_id=0, has_side_effects=True, vmem_limit_bytes=16 * MIB
        ),
    )(plan, state, mask)


def leaves(plan_ref, chips, chip, t, way):
    target = plan_ref[4 * chip + t] // 4
    return target == lax.rem(chip + way + chips, chips)


def pick(index, values):
    chosen = values[0]
    for at, value in enumerate(values[1:], 1):
        chosen = jnp.where(index == at, value, chosen)
    return chosen


def move_kernel(
    rounds,
    idle,
    plan_ref,
    state_ref,
    diff_ref,
    mask_ref,
    lat_ref,
    west_ref,
    east_ref,
    out_ref,
    padded,
    wet,
    mine,
    theirs,
    other,
    other_theirs,
    leaving,
    arrived,
    swapped,
    relayed,
    result,
    load_sem,
    store_sem,
    half_send,
    half_recv,
    tile_send,
    tile_recv,
    swap_send,
    swap_recv,
    relay_send,
    relay_recv,
):
    fields, levels, rows, lanes = state_ref.shape
    planes = fields * levels
    quarter = rows // 4
    chunks = quarter // STEP
    devices, bands = lax.axis_size("lon"), lax.axis_size("lat")
    chips = devices // 2
    tiles = 4 * chips
    lon, lat = lax.axis_index("lon"), lax.axis_index("lat")
    chip, core = lon // 2, lax.rem(lon, 2)
    twin = {"lon": lon + 1 - 2 * core}
    ahead_lon = lax.rem(lon + 2, devices)
    behind_lon = lax.rem(lon + devices - 2, devices)
    ways = ((1, ahead_lon), (-1, behind_lon))
    keys = [(side, r) for side in range(2) for r in range(rounds)]
    active = None if idle is None else lat != idle

    def busy(work):
        if idle is None:
            work()
        else:
            pl.when(active)(work)

    def resting(work):
        if idle is not None:
            pl.when(lat == idle)(work)

    loads = [
        pltpu.make_async_copy(state_ref.at[f], padded.at[f, :, pl.ds(8, rows), :], load_sem.at[f])
        for f in range(fields)
    ]
    barrier = pltpu.get_barrier_semaphore()

    def greet(who):
        pl.semaphore_signal(barrier, inc=1, device_id=who, device_id_type=MESH)

    greet(twin)

    @busy
    def _():
        greet({"lon": ahead_lon})
        greet({"lon": behind_lon})
        if idle is not None:
            for at in (lon, ahead_lon, behind_lon):
                greet({"lat": idle, "lon": at})

    @resting
    def _():
        for o in range(1, bands):
            for at in (lon, ahead_lon, behind_lon):
                greet({"lat": (idle + o) % bands, "lon": at})

    for load in loads:
        load.start()

    wet[pl.ds(8, rows), :] = mask_ref[...].astype(F32)
    wet[0:8, :] = jnp.ones((8, lanes), F32)
    wet[rows + 8 : rows + 16, :] = jnp.ones((8, lanes), F32)
    for f in range(fields):
        for k in range(levels):
            i = f * levels + k
            padded[f, k, 7:8, :] = west_ref[i : i + 1, :]
            padded[f, k, rows + 8 : rows + 9, :] = east_ref[i : i + 1, :]

    chosen = {}
    for side, (way, _) in enumerate(ways):
        hits = [leaves(plan_ref, chips, chip, t, way) for t in range(4)]
        for r in range(rounds):
            count, tile = jnp.int32(0), jnp.int32(0)
            for t in range(4):
                tile = jnp.where(hits[t] & (count == r), t, tile)
                count = count + hits[t].astype(jnp.int32)
            chosen[side, r] = jnp.where(tile // 2 == core, 0, 2) + lax.rem(tile, 2)

    lane = lax.broadcasted_iota(jnp.int32, (STEP, lanes), 1)
    is_last = lane == lanes - 1
    is_first = lane == 0
    force = gradient_coef * weight_coef

    def solve(c, half, to_ref):
        def group(slot, _):
            row = pl.multiple_of(half * quarter + c * STEP, STEP)
            base = pl.multiple_of(slot * (2 * quarter) + row, STEP)
            edges = pltpu.roll(lat_ref[pl.ds(row, STEP), :], 64 * slot, 1)
            wet_c = wet[pl.ds(base + 8, STEP), :]
            wet_e = wet[pl.ds(base + 9, STEP), :]
            wet_w = wet[pl.ds(base + 7, STEP), :]
            zonal = meridional = None
            upper = []
            rhs = []
            for k in range(levels):
                center = [padded[f, k, pl.ds(base + 8, STEP), :] * wet_c for f in range(fields)]
                u, v = center[2], center[3]
                grad_x, grad_y, value = [], [], []
                for f in range(fields):
                    i = f * levels + k
                    e = padded[f, k, pl.ds(base + 9, STEP), :] * wet_e
                    w = padded[f, k, pl.ds(base + 7, STEP), :] * wet_w
                    edge = pltpu.roll(edges, (lanes - 2 - 2 * i) % lanes, 1)
                    n = jnp.where(is_last, edge, pltpu.roll(center[f], lanes - 1, 1))
                    s = jnp.where(is_first, edge, pltpu.roll(center[f], 1, 1))
                    gx, gy = e - w, n - s
                    grad_x.append(gx)
                    grad_y.append(gy)
                    total = (e + w) + (n + s)
                    flow = u * gx + v * gy
                    value.append(
                        (1.0 - 4.0 * diffuse_coef) * center[f] + (diffuse_coef * total - advect_coef * flow)
                    )
                dx = (force * haline_coef) * grad_x[1] - (force * thermal_coef) * grad_x[0]
                dy = (force * haline_coef) * grad_y[1] - (force * thermal_coef) * grad_y[0]
                zonal = dx if k == 0 else zonal + dx
                meridional = dy if k == 0 else meridional + dy
                value[2] = value[2] - zonal
                value[3] = value[3] - meridional
                lower_k = diff_ref[k - 1, pl.ds(base, STEP), :] if k > 0 else None
                upper_k = diff_ref[k, pl.ds(base, STEP), :] if k < levels - 1 else None
                pivot = 1.0
                if k > 0:
                    pivot = pivot + lower_k
                if k < levels - 1:
                    pivot = pivot + upper_k
                if k > 0:
                    pivot = pivot - lower_k * upper[k - 1]
                inverse = 1.0 / pivot
                upper.append(upper_k * inverse if k < levels - 1 else None)
                if k > 0:
                    value = [value[f] + lower_k * rhs[k - 1][f] for f in range(fields)]
                rhs.append([value[f] * inverse for f in range(fields)])
            for f in range(fields):
                x = rhs[levels - 1][f]
                to_ref[c, slot, f * levels + levels - 1] = x * wet_c
                for k in range(levels - 2, -1, -1):
                    x = rhs[k][f] + upper[k] * x
                    to_ref[c, slot, f * levels + k] = x * wet_c
            return 0

        lax.fori_loop(0, 2, group, 0)

    def first(c):
        return remote_copy(theirs.at[c], other.at[c], half_send.at[c, 0], half_recv.at[c, 0], twin)

    def second(c):
        return remote_copy(mine.at[c], other_theirs.at[c], half_send.at[c, 1], half_recv.at[c, 1], twin)

    def direct(c, side, r):
        return remote_copy(
            leaving.at[side, r, c],
            arrived.at[side, r, c],
            tile_send.at[c, side, r],
            tile_recv.at[c, side, r],
            {"lon": ways[side][1]},
        )

    def swap(c, side, r):
        return remote_copy(
            arrived.at[side, r, c],
            swapped.at[side, r, c],
            swap_send.at[c, side, r],
            swap_recv.at[c, side, r],
            twin,
        )

    stops = [(side, n, c) for side, cs in enumerate(RELAYED) for n, c in enumerate(cs)] if idle is not None else []
    stops.sort(key=lambda stop: stop[2])

    def detour(at, side, c):
        j = lax.rem(lat - (idle + 1) + 2 * bands, bands)
        return remote_copy(
            leaving.at[side, 0, c],
            relayed.at[j, at],
            tile_send.at[c, side, 0],
            relay_recv.at[j, at],
            {"lat": idle, "lon": ways[side][1]},
        )

    def forward(j, at, side, c):
        return remote_copy(
            relayed.at[j, at],
            arrived.at[side, 0, c],
            relay_send.at[j, at],
            tile_recv.at[c, side, 0],
            {"lat": (idle + 1 + j) % bands},
        )

    for load in loads:
        load.wait()

    def advance(c, _):
        solve(c, 1 - core, theirs)

        @pl.when(c == 0)
        def _():
            if idle is None:
                pl.semaphore_wait(barrier, 3)
            else:
                busy(lambda: pl.semaphore_wait(barrier, 6))
                resting(lambda: pl.semaphore_wait(barrier, 1 + 3 * (bands - 1)))

        first(c).start()
        solve(c, core, mine)

        @busy
        def _():
            first(c).wait_recv()

            def pack(i, _):
                held = [ref[c, slot, i] for ref in (mine, other) for slot in range(2)]
                for (side, r), index in chosen.items():
                    leaving[side, r, c, i] = pick(index, held)
                return 0

            lax.fori_loop(0, planes, pack, 0, unroll=8)
            for side, r in keys:
                around = [c == stop[2] for stop in stops if stop[0] == side]
                if around:
                    pl.when(jnp.logical_not(functools.reduce(jnp.logical_or, around)))(direct(c, side, r).start)
                else:
                    direct(c, side, r).start()
            for at, (side, _, when) in enumerate(stops):
                pl.when(c == when)(detour(at, side, when).start)

        second(c).start()
        return 0

    lax.fori_loop(0, chunks, advance, 0)

    @resting
    def _():
        for at, (side, _, c) in enumerate(stops):
            for j in range(bands - 1):
                remote_copy(
                    relayed.at[j, at], relayed.at[j, at], relay_send.at[j, at], relay_recv.at[j, at], twin
                ).wait_recv()
                forward(j, at, side, c).start()

    origin = []
    for slot in range(2):
        target = 2 * lon + slot
        source = jnp.int32(0)
        for shift in range(-3, 4):
            g = lax.rem(target + shift + tiles, tiles)
            source = jnp.where(plan_ref[g] == target, g, source)
        from_chip, t = source // 4, lax.rem(source, 4)
        at = jnp.where(t // 2 == core, 0, 2) + lax.rem(t, 2)
        for side, (way, _) in enumerate(ways):
            came = from_chip == lax.rem(chip - way + chips, chips)
            rank = jnp.int32(0)
            for q in range(3):
                hit = leaves(plan_ref, chips, from_chip, q, way) & (q < t)
                rank = rank + hit.astype(jnp.int32)
            at = jnp.where(came, 4 + side * rounds + jnp.minimum(rank, rounds - 1), at)
        origin.append(at)

    def store(c, slot, part):
        half = core if part == 0 else 1 - core
        row = pl.multiple_of(2 * quarter * slot + half * quarter + c * STEP, STEP)
        return pltpu.make_async_copy(
            result.at[c, slot, part], out_ref.at[:, :, pl.ds(row, STEP), :], store_sem.at[c, slot, part]
        )

    def place(c):
        second(c).wait_recv()
        resting(first(c).wait_recv)

        @busy
        def _():
            for key in keys:
                swap(c, *key).wait_recv()

        def level(k, _):
            for f in range(fields):
                i = f * levels + k
                for part in range(2):
                    near, far, came = (
                        (mine, other, arrived) if part == 0 else (theirs, other_theirs, swapped)
                    )
                    values = [ref[c, slot, i] for ref in (near, far) for slot in range(2)]
                    values += [came[side, r, c, i] for side, r in keys]
                    for slot in range(2):
                        result[c, slot, part, f, k] = pick(origin[slot], values)
            return 0

        lax.fori_loop(0, levels, level, 0)
        for slot in range(2):
            for part in range(2):
                store(c, slot, part).start()

    def drain(c, _):
        @busy
        def _():
            for key in keys:
                direct(c, *key).wait_recv()
                swap(c, *key).start()

        @pl.when(c > 0)
        def _():
            place(c - 1)

        return 0

    lax.fori_loop(0, chunks, drain, 0)
    place(chunks - 1)

    def finish(c, _):
        first(c).wait_send()
        second(c).wait_send()

        @busy
        def _():
            for key in keys:
                direct(c, *key).wait_send()
                swap(c, *key).wait_send()

        for slot in range(2):
            for part in range(2):
                store(c, slot, part).wait()
        return 0

    lax.fori_loop(0, chunks, finish, 0)

    @resting
    def _():
        for at, (side, _, c) in enumerate(stops):
            for j in range(bands - 1):
                forward(j, at, side, c).wait_send()


def move(rounds, idle, plan, state, diffusivity, mask, lat_edges, west, east):
    fields, levels, rows, lanes = state.shape
    bands = lax.axis_size("lat")
    chunks = rows // 4 // STEP
    planes = fields * levels
    stops = sum(len(cs) for cs in RELAYED)
    anywhere = pl.BlockSpec(memory_space=pl.ANY)
    near = pl.BlockSpec(memory_space=pltpu.VMEM)
    halves = pltpu.VMEM((chunks, 2, planes, STEP, lanes), F32)
    pieces = pltpu.VMEM((2, rounds, chunks, planes, STEP, lanes), F32)
    relay_shape = (bands - 1, stops) if idle is not None else (1, 1)
    dma = pltpu.SemaphoreType.DMA
    number = rounds if idle is None else 4 + idle
    return pl.pallas_call(
        functools.partial(move_kernel, rounds, idle),
        in_specs=[pl.BlockSpec(memory_space=pltpu.SMEM), anywhere] + [near] * 5,
        out_specs=anywhere,
        out_shape=jax.ShapeDtypeStruct(state.shape, F32),
        scratch_shapes=[
            pltpu.VMEM((fields, levels, rows + 16, lanes), F32),
            pltpu.VMEM((rows + 16, lanes), F32),
            halves,
            halves,
            halves,
            halves,
            pieces,
            pieces,
            pieces,
            pltpu.VMEM(relay_shape + (planes, STEP, lanes), F32),
            pltpu.VMEM((chunks, 2, 2, fields, levels, STEP, lanes), F32),
            dma((fields,)),
            dma((chunks, 2, 2)),
            dma((chunks, 2)),
            dma((chunks, 2)),
            dma((chunks, 2, rounds)),
            dma((chunks, 2, rounds)),
            dma((chunks, 2, rounds)),
            dma((chunks, 2, rounds)),
            dma(relay_shape),
            dma(relay_shape),
        ],
        compiler_params=pltpu.CompilerParams(
            collective_id=number, has_side_effects=True, vmem_limit_bytes=(24 + 6 * rounds) * MIB
        ),
    )(plan, state, diffusivity, mask, lat_edges, west, east)


def local(relays, state, diffusivity, mask, tile_plan):
    plan = tile_plan.reshape(-1)
    lat_edges, west, east, branch = halos(relays, plan, state, mask)
    branches = [functools.partial(move, rounds, None) for rounds in (1, 2, 3)]
    if relays:
        branches = [functools.partial(move, 1, row) for row in range(lax.axis_size("lat"))] + branches
    return lax.switch(branch[0], branches, plan, state, diffusivity, mask, lat_edges, west, east)


def solution(mesh):
    placed = (P(None, None, "lon", "lat"), P(None, "lon", "lat"), P("lon", "lat"), P(None, "lat"))
    relays = False
    return jax.shard_map(
        functools.partial(local, relays),
        mesh=mesh,
        in_specs=placed,
        out_specs=P(None, None, "lon", "lat"),
        check_vma=False,
    )
```

profile of v0, /device:TPU:1, one launch (start us, length us, event | category | flops | bytes accessed | tf_op | source)
XLA Modules:
  0.0 70.4 jit_solution(14940922497602316870)
XLA Ops:
  0.0 0.0 copy-start.1
  0.0 0.0 copy-start
  0.0 0.0 copy-start.2
  0.0 12.8 %shard_map.49 = (f32[128,128]{1,0:T(8,128)S(1)}, f32[32,128]{1,0:T(8,128)S(1)}, f32[32,128]{1,0:T(8,128)S(1)}, s32[1]{0:T(128)}) custom-call(s32[16]{0:T(128)} %bitcast.2, f32[4,8,256,128]{3,2,1,0:T(8,128)} %state_ref.1, s32[256,128]{1,0:T(8,128)} %mask_ref.1), custom_call_target="tpu_custom_call" | custom-call | tf_op jit(solution)/shard_map/pallas_call | solution.py:192
  13.4 0.0 copy-done.1
  13.4 0.0 copy-done
  13.4 0.0 copy-done.2
  13.4 55.0 %conditional.1 = (f32[4,8,256,128]{3,2,1,0:T(8,128)S(1)}) conditional(s32[]{:T(128)} %bitcast.1, (s32[16]{0:T(128)S(1)}, f32[4,8,256,128]{3,2,1,0:T(8,128)S(1)}, f32[7,256,128]{2,1,0:T(8,128)}, s32[256,128]{1,0:T(8,128)S(1)}, f32[128,128]{1,0:T(8,128)S(1)}, /*index=5*/f32[32,128]{1,0:T(8,128)S(1)}, ...), branch_computations={%region_0.0_spmd, %region_1.0_spmd, %region_2.0_spmd} | conditional | bytes 8 | solution.py:648
  13.4 54.9 %branch_0_fun.1 = f32[4,8,256,128]{3,2,1,0:T(8,128)S(1)} custom-call(s32[16]{0:T(128)S(1)} %get-tuple-element.50.plan_ref, f32[4,8,256,128]{3,2,1,0:T(8,128)S(1)} %get-tuple-element.52.state_ref, f32[7,256,128]{2,1,0:T(8,128)} %get-tuple-element.53.diff_ref, s32[256,128]{1,0:T(8,128)S(1)} %get-tuple-element.54.mask_ref, ...), custom_call_target="tpu_custom_call" | custom-call | tf_op jit(solution)/shard_map/cond/branch_0_fun/pallas_call | solution.py:608
  68.4 2.0 %copy.12 = f32[4,8,256,128]{3,2,1,0:T(8,128)} copy(f32[4,8,256,128]{3,2,1,0:T(8,128)S(1)} %get-tuple-element.80) | data formatting | bytes 8388608
Async XLA Ops:
  0.0 13.4 %copy-start.1 = (s32[256,128]{1,0:T(8,128)S(1)}, s32[256,128]{1,0:T(8,128)}, u32[]{:S(2)}) copy-start(s32[256,128]{1,0:T(8,128)} %mask_ref.1) | copy-start | bytes 393220
  0.0 13.4 %copy-start = (f32[4,8,256,128]{3,2,1,0:T(8,128)S(1)}, f32[4,8,256,128]{3,2,1,0:T(8,128)}, u32[]{:S(2)}) copy-start(f32[4,8,256,128]{3,2,1,0:T(8,128)} %state_ref.1) | copy-start | bytes 12582916
  0.0 13.4 %copy-start.2 = (s32[16,1]{0,1:T(1,128)S(1)}, s32[16,1]{0,1:T(1,128)}, u32[]{:S(2)}) copy-start(s32[16,1]{0,1:T(1,128)} %param.10) | copy-start | bytes 196
where the time goes:
time: 70.6 us; the launch traced here: 70.4 us
  Pallas kernels  67.7 us (96%)
  local copies, waits for them, and re-layouts  2.03 us (3%)
    pallas_call x1, Pallas kernels, move(): pl.pallas_call(functools.partial(move_kernel, rounds, idle), in_specs=[pl...  54.9 us
    pallas_call x1, Pallas kernels, halos(): pl.pallas_call(functools.partial(halo_kernel, relays), in_specs=[scalars,...  12.8 us
    unnamed x7, local copies, waits for them, and re-layouts  2.03 us

commit v1 on v0

--- a/solution.py
+++ b/solution.py
@@ -18,7 +18,7 @@
 MIB = 1 << 20
 MESH = pl.DeviceIdType.MESH
 STEP = 8
-RELAYED = ((1, 4), (2,))
+RELAYED = 2
 
 
 def remote_copy(source, target, send, recv, who):
@@ -262,6 +262,8 @@
     tile_recv,
     swap_send,
     swap_recv,
+    leg_send,
+    leg_recv,
     relay_send,
     relay_recv,
 ):
@@ -409,10 +411,10 @@
     def second(c):
         return remote_copy(mine.at[c], other_theirs.at[c], half_send.at[c, 1], half_recv.at[c, 1], twin)
 
-    def direct(c, side, r):
+    def direct(c, side, r, part):
         return remote_copy(
-            leaving.at[side, r, c],
-            arrived.at[side, r, c],
+            leaving.at[side, r, c, part],
+            arrived.at[side, r, c, part],
             tile_send.at[c, side, r],
             tile_recv.at[c, side, r],
             {"lon": ways[side][1]},
@@ -427,27 +429,72 @@
             twin,
         )
 
-    stops = [(side, n, c) for side, cs in enumerate(RELAYED) for n, c in enumerate(cs)] if idle is not None else []
-    stops.sort(key=lambda stop: stop[2])
-
-    def detour(at, side, c):
+    relay_chunks = chunks // 2
+    relays = RELAYED * relay_chunks - 1
+
+    def part_of(n):
+        return n // RELAYED, pl.ds(lax.rem(n, RELAYED) * levels, levels)
+
+    def detour(side, n):
         j = lax.rem(lat - (idle + 1) + 2 * bands, bands)
+        c, part = part_of(n)
         return remote_copy(
-            leaving.at[side, 0, c],
-            relayed.at[j, at],
-            tile_send.at[c, side, 0],
-            relay_recv.at[j, at],
+            leaving.at[side, 0, c, part],
+            relayed.at[j, side, n],
+            leg_send.at[side, n],
+            leg_recv.at[j, side, n],
             {"lat": idle, "lon": ways[side][1]},
         )
 
-    def forward(j, at, side, c):
+    def forward(j, side, n):
+        c, part = part_of(n)
         return remote_copy(
-            relayed.at[j, at],
-            arrived.at[side, 0, c],
-            relay_send.at[j, at],
-            tile_recv.at[c, side, 0],
-            {"lat": (idle + 1 + j) % bands},
+            relayed.at[j, side, n],
+            arrived.at[side, 0, c, part],
+            relay_send.at[j, side, n],
+            relay_recv.at[side, n],
+            {"lat": lax.rem(idle + 1 + j, bands)},
         )
+
+    def pass_on(t):
+        groups = []
+        if idle is not None:
+            above, below = list(range(bands - 1, idle, -1)), list(range(idle))
+            while above or below:
+                groups.append([rows.pop(0) for rows in (above, below) if rows])
+        before, j, n = 0, jnp.int32(0), jnp.int32(0)
+        for group in groups:
+            at = t - before
+            inside = at >= 0
+            which = [(row - idle - 1) % bands for row in group]
+            j = jnp.where(inside, pick(lax.rem(jnp.maximum(at, 0), len(group)), which), j)
+            n = jnp.where(inside, jnp.maximum(at, 0) // len(group), n)
+            before += relays * len(group)
+        for side in range(2):
+            here(j, side, n).wait_recv()
+            forward(j, side, n).start()
+
+    def here(j, side, n):
+        return remote_copy(
+            relayed.at[j, side, n], relayed.at[j, side, n], relay_send.at[j, side, n], leg_recv.at[j, side, n], twin
+        )
+
+    def each_part(c, work):
+        if idle is None:
+            work(slice(0, planes))
+            return
+        pl.when(c < relay_chunks - 1)(lambda: work(pl.ds(RELAYED * levels, planes - RELAYED * levels)))
+        pl.when(c == relay_chunks - 1)(
+            lambda: work(pl.ds((RELAYED - 1) * levels, planes - (RELAYED - 1) * levels))
+        )
+        pl.when(c >= relay_chunks)(lambda: work(slice(0, planes)))
+
+    def each_relay(c, work):
+        if idle is None:
+            return
+        for f in range(RELAYED):
+            n = c * RELAYED + f
+            pl.when(n < relays)(functools.partial(work, n))
 
     for load in loads:
         load.wait()
@@ -477,28 +524,28 @@
                 return 0
 
             lax.fori_loop(0, planes, pack, 0, unroll=8)
-            for side, r in keys:
-                around = [c == stop[2] for stop in stops if stop[0] == side]
-                if around:
-                    pl.when(jnp.logical_not(functools.reduce(jnp.logical_or, around)))(direct(c, side, r).start)
-                else:
-                    direct(c, side, r).start()
-            for at, (side, _, when) in enumerate(stops):
-                pl.when(c == when)(detour(at, side, when).start)
+            def relay(n):
+                for side in range(2):
+                    detour(side, n).start()
+
+            def send(part):
+                for side, r in keys:
+                    direct(c, side, r, part).start()
+
+            each_relay(c, relay)
+            each_part(c, send)
 
         second(c).start()
+
+        @resting
+        def _():
+            @pl.when(c > 0)
+            def _():
+                pass_on(c - 1)
+
         return 0
 
     lax.fori_loop(0, chunks, advance, 0)
-
-    @resting
-    def _():
-        for at, (side, _, c) in enumerate(stops):
-            for j in range(bands - 1):
-                remote_copy(
-                    relayed.at[j, at], relayed.at[j, at], relay_send.at[j, at], relay_recv.at[j, at], twin
-                ).wait_recv()
-                forward(j, at, side, c).start()
 
     origin = []
     for slot in range(2):
@@ -552,21 +599,47 @@
             for part in range(2):
                 store(c, slot, part).start()
 
-    def drain(c, _):
+    def chunk_at(step):
+        if idle is None:
+            return step
+        return step // 2 + relay_chunks * lax.rem(step, 2)
+
+    left = (bands - 1) * relays - (chunks - 1)
+    each_step = -(-left // chunks)
+
+    def drain(step, _):
         @busy
         def _():
-            for key in keys:
-                direct(c, *key).wait_recv()
-                swap(c, *key).start()
-
-        @pl.when(c > 0)
+            @pl.when(step < chunks)
+            def _():
+                c = chunk_at(step)
+
+                def receive(part):
+                    for key in keys:
+                        direct(c, *key, part).wait_recv()
+
+                def receive_relay(n):
+                    for side in range(2):
+                        forward(0, side, n).wait_recv()
+
+                each_part(c, receive)
+                each_relay(c, receive_relay)
+                for key in keys:
+                    swap(c, *key).start()
+
+        @resting
         def _():
-            place(c - 1)
+            for more in range(each_step):
+                t = step * each_step + more
+                pl.when(t < left)(lambda: pass_on(chunks - 1 + t))
+
+        @pl.when(step > 0)
+        def _():
+            place(chunk_at(step - 1))
 
         return 0
 
-    lax.fori_loop(0, chunks, drain, 0)
-    place(chunks - 1)
+    lax.fori_loop(0, chunks + 1, drain, 0)
 
     def finish(c, _):
         first(c).wait_send()
@@ -574,8 +647,17 @@
 
         @busy
         def _():
+            def sent(part):
+                for key in keys:
+                    direct(c, *key, part).wait_send()
+
+            def sent_relay(n):
+                for side in range(2):
+                    detour(side, n).wait_send()
+
+            each_part(c, sent)
+            each_relay(c, sent_relay)
             for key in keys:
-                direct(c, *key).wait_send()
                 swap(c, *key).wait_send()
 
         for slot in range(2):
@@ -587,9 +669,13 @@
 
     @resting
     def _():
-        for at, (side, _, c) in enumerate(stops):
-            for j in range(bands - 1):
-                forward(j, at, side, c).wait_send()
+        def relay_sent(n, _):
+            for side in range(2):
+                for j in range(bands - 1):
+                    forward(j, side, n).wait_send()
+            return 0
+
+        lax.fori_loop(0, relays, relay_sent, 0)
 
 
 def move(rounds, idle, plan, state, diffusivity, mask, lat_edges, west, east):
@@ -597,12 +683,12 @@
     bands = lax.axis_size("lat")
     chunks = rows // 4 // STEP
     planes = fields * levels
-    stops = sum(len(cs) for cs in RELAYED)
+    relays = RELAYED * (chunks // 2) - 1 if idle is not None else 1
+    others = bands - 1 if idle is not None else 1
     anywhere = pl.BlockSpec(memory_space=pl.ANY)
     near = pl.BlockSpec(memory_space=pltpu.VMEM)
     halves = pltpu.VMEM((chunks, 2, planes, STEP, lanes), F32)
     pieces = pltpu.VMEM((2, rounds, chunks, planes, STEP, lanes), F32)
-    relay_shape = (bands - 1, stops) if idle is not None else (1, 1)
     dma = pltpu.SemaphoreType.DMA
     number = rounds if idle is None else 4 + idle
     return pl.pallas_call(
@@ -620,7 +706,7 @@
             pieces,
             pieces,
             pieces,
-            pltpu.VMEM(relay_shape + (planes, STEP, lanes), F32),
+            pltpu.VMEM((others, 2, relays, levels, STEP, lanes), F32),
             pltpu.VMEM((chunks, 2, 2, fields, levels, STEP, lanes), F32),
             dma((fields,)),
             dma((chunks, 2, 2)),
@@ -630,8 +716,10 @@
             dma((chunks, 2, rounds)),
             dma((chunks, 2, rounds)),
             dma((chunks, 2, rounds)),
-            dma(relay_shape),
-            dma(relay_shape),
+            dma((2, relays)),
+            dma((others, 2, relays)),
+            dma((others, 2, relays)),
+            dma((2, relays)),
         ],
         compiler_params=pltpu.CompilerParams(
             collective_id=number, has_side_effects=True, vmem_limit_bytes=(24 + 6 * rounds) * MIB
@@ -650,7 +738,7 @@
 
 def solution(mesh):
     placed = (P(None, None, "lon", "lat"), P(None, "lon", "lat"), P("lon", "lat"), P(None, "lat"))
-    relays = False
+    relays = mesh.shape["lat"] == 4
     return jax.shard_map(
         functools.partial(local, relays),
         mesh=mesh,

time: 70.6 us -> 63.1 us (0.89)
  Pallas kernels: 67.7 us -> 60.2 us
    pallas_call x1, Pallas kernels: 54.9 us -> 47.4 us  [move(): pl.pallas_call(functools.partial(move_kernel, rounds, idle), in_specs=[pl...]
where the time goes in v1:
time: 63.1 us; the launch traced here: 62.9 us
  Pallas kernels  60.2 us (95%)
  local copies, waits for them, and re-layouts  2.03 us (3%)
  between operations  0.67 us (1%)
    pallas_call x1, Pallas kernels, move(): pl.pallas_call(functools.partial(move_kernel, rounds, idle), in_specs=[pl...  47.4 us
    pallas_call x1, Pallas kernels, halos(): pl.pallas_call(functools.partial(halo_kernel, relays), in_specs=[scalars,...  12.8 us
    unnamed x7, local copies, waits for them, and re-layouts  2.03 us

profile of v1, /device:TPU:1, one launch (start us, length us, event | category | flops | bytes accessed | tf_op | source)
XLA Modules:
  0.0 62.9 jit_solution(17179622372120306149)
XLA Ops:
  0.0 0.0 copy-start.1
  0.0 0.0 copy-start
  0.0 0.0 copy-start.2
  0.0 12.8 %shard_map.53 = (f32[128,128]{1,0:T(8,128)S(1)}, f32[32,128]{1,0:T(8,128)S(1)}, f32[32,128]{1,0:T(8,128)S(1)}, s32[1]{0:T(128)}) custom-call(s32[16]{0:T(128)} %bitcast.2, f32[4,8,256,128]{3,2,1,0:T(8,128)} %state_ref.1, s32[256,128]{1,0:T(8,128)} %mask_ref.1), custom_call_target="tpu_custom_call" | custom-call | tf_op jit(solution)/shard_map/pallas_call | solution.py:192
  13.4 0.0 copy-done.1
  13.4 0.0 copy-done
  13.5 0.0 copy-done.2
  13.5 47.4 %conditional.1 = (f32[4,8,256,128]{3,2,1,0:T(8,128)S(1)}) conditional(s32[]{:T(128)} %bitcast.1, (s32[16]{0:T(128)S(1)}, f32[4,8,256,128]{3,2,1,0:T(8,128)S(1)}, f32[7,256,128]{2,1,0:T(8,128)}, s32[256,128]{1,0:T(8,128)S(1)}, f32[128,128]{1,0:T(8,128)S(1)}, /*index=5*/f32[32,128]{1,0:T(8,128)S(1)}, ...), branch_computations={%region_0.0_spmd, %region_1.0_spmd, %region_2.0_spmd, %region_3.0_... | conditional | bytes 8 | solution.py:736
  13.5 47.4 %branch_3_fun.1 = f32[4,8,256,128]{3,2,1,0:T(8,128)S(1)} custom-call(s32[16]{0:T(128)S(1)} %get-tuple-element.132.plan_ref, f32[4,8,256,128]{3,2,1,0:T(8,128)S(1)} %get-tuple-element.133.state_ref, f32[7,256,128]{2,1,0:T(8,128)} %get-tuple-element.134.diff_ref, s32[256,128]{1,0:T(8,128)S(1)} %get-tuple-element.135.mask_ref, ...), custom_call_target="tpu_custom_call" | custom-call | tf_op jit(solution)/shard_map/cond/branch_3_fun/pallas_call | solution.py:694
  60.9 2.0 %copy.20 = f32[4,8,256,128]{3,2,1,0:T(8,128)} copy(f32[4,8,256,128]{3,2,1,0:T(8,128)S(1)} %get-tuple-element.168) | data formatting | bytes 8388608
Async XLA Ops:
  0.0 13.4 %copy-start.1 = (s32[256,128]{1,0:T(8,128)S(1)}, s32[256,128]{1,0:T(8,128)}, u32[]{:S(2)}) copy-start(s32[256,128]{1,0:T(8,128)} %mask_ref.1) | copy-start | bytes 393220
  0.0 13.4 %copy-start = (f32[4,8,256,128]{3,2,1,0:T(8,128)S(1)}, f32[4,8,256,128]{3,2,1,0:T(8,128)}, u32[]{:S(2)}) copy-start(f32[4,8,256,128]{3,2,1,0:T(8,128)} %state_ref.1) | copy-start | bytes 12582916
  0.0 13.5 %copy-start.2 = (s32[16,1]{0,1:T(1,128)S(1)}, s32[16,1]{0,1:T(1,128)}, u32[]{:S(2)}) copy-start(s32[16,1]{0,1:T(1,128)} %param.14) | copy-start | bytes 196

commit v2 on v1

--- a/solution.py
+++ b/solution.py
@@ -18,6 +18,7 @@
 MIB = 1 << 20
 MESH = pl.DeviceIdType.MESH
 STEP = 8
+RELAYS = 7
 RELAYED = 2
 
 
@@ -32,11 +33,12 @@
     plan_ref,
     state_ref,
     mask_ref,
+    diff_ref,
     lat_ref,
-    west_ref,
-    east_ref,
+    padded,
+    wet,
+    diff_out,
     branch_ref,
-    held,
     mask,
     lat_pack,
     lon_pack,
@@ -50,8 +52,10 @@
     send_sem,
     recv_sem,
 ):
-    fields, levels, rows, lanes = held.shape
-    half = rows // 2
+    fields, levels, rows, lanes = state_ref.shape
+    half, quarter = rows // 2, rows // 4
+    pairs = fields // 2
+    width = lanes // 4
     lane = lax.broadcasted_iota(jnp.int32, (8, lanes), 1)
     devices, bands = lax.axis_size("lon"), lax.axis_size("lat")
     lon, lat = lax.axis_index("lon"), lax.axis_index("lat")
@@ -66,9 +70,14 @@
 
     mask_load = pltpu.make_async_copy(mask_ref, mask, load_sem.at[fields])
     mask_load.start()
-    loads = [pltpu.make_async_copy(state_ref.at[f], held.at[f], load_sem.at[f]) for f in range(fields)]
+    loads = [
+        pltpu.make_async_copy(state_ref.at[f], padded.at[f, :, pl.ds(8, rows), :], load_sem.at[f])
+        for f in range(fields)
+    ]
     for load in loads:
         load.start()
+    diff_load = pltpu.make_async_copy(diff_ref, diff_out, load_sem.at[fields + 1])
+    diff_load.start()
 
     chips = devices // 2
 
@@ -82,48 +91,64 @@
 
     most = lax.fori_loop(0, chips, leaving, jnp.int32(0))
     count[...] = jnp.full(count.shape, most, jnp.int32)
-    mask_load.wait()
-    first = mask[0:1, :].astype(F32)
-    final = mask[rows - 1 : rows, :].astype(F32)
-    for f in range(fields):
-        loads[f].wait()
-
-        def group(g, _):
-            to = pl.ds(pl.multiple_of(g * 8, 8), 8)
-            part = lat_pack[to, :] if f > 0 else jnp.zeros((8, lanes), F32)
-            for slot in range(2):
-                at = pl.ds(pl.multiple_of(slot * half + g * 8, 8), 8)
-                wet = mask[at, :].astype(F32)
-                for k in range(levels):
-                    place = 64 * slot + 2 * (f * levels + k)
-                    x = pltpu.roll(held[f, k, at, :] * wet, place + 1, 1)
-                    part = jnp.where((lane >> 1) == (place >> 1), x, part)
-            lat_pack[to, :] = part
-            return 0
-
-        lax.fori_loop(0, half // 8, group, 0, unroll=2)
-        at_field = slice(f * levels, (f + 1) * levels)
-        lon_pack[0, at_field, :] = jnp.concatenate([held[f, k, 0:1, :] for k in range(levels)], 0) * first
-        lon_pack[1, at_field, :] = (
-            jnp.concatenate([held[f, k, rows - 1 : rows, :] for k in range(levels)], 0) * final
-        )
-
-    pl.semaphore_wait(barrier, 3 + bands - 1)
 
     def remote(source, target, at, recv_at, who):
         return remote_copy(source, target, send_sem.at[at], recv_sem.at[recv_at], who)
 
-    up = remote(lat_pack, south_in, 0, 0, {"lat": jnp.minimum(lat + 1, bands - 1)})
-    down = remote(lat_pack, north_in, 1, 1, {"lat": jnp.maximum(lat - 1, 0)})
-    fold = remote(lat_pack, north_in, 0, 1, across)
-    east = remote(lon_pack.at[1], west_in, 2, 2, to_east)
-    west = remote(lon_pack.at[0], east_in, 3, 3, to_west)
-    tell = [remote(count, counts_in.at[o], 4 + o, 4 + o, who) for o, who in enumerate(others)]
-    pl.when(top)(fold.start)
-    pl.when(jnp.logical_not(top))(up.start)
-    pl.when(lat > 0)(down.start)
+    north_who, south_who = {"lat": jnp.minimum(lat + 1, bands - 1)}, {"lat": jnp.maximum(lat - 1, 0)}
+    up = [remote(lat_pack.at[q], south_in.at[q], q, q, north_who) for q in range(pairs)]
+    down = [remote(lat_pack.at[q], north_in.at[q], pairs + q, pairs + q, south_who) for q in range(pairs)]
+    fold = [remote(lat_pack.at[q], north_in.at[q], q, pairs + q, across) for q in range(pairs)]
+    at_lon = 2 * pairs
+    east = remote(lon_pack.at[1], west_in, at_lon, at_lon, to_east)
+    west = remote(lon_pack.at[0], east_in, at_lon + 1, at_lon + 1, to_west)
+    tell = [
+        remote(count, counts_in.at[o], at_lon + 2 + o, at_lon + 2 + o, who) for o, who in enumerate(others)
+    ]
+    pl.semaphore_wait(barrier, 3 + bands - 1)
     for t in tell:
         t.start()
+    mask_load.wait()
+    wet[pl.ds(8, rows), :] = mask[...].astype(F32)
+    wet[0:8, :] = jnp.ones((8, lanes), F32)
+    wet[rows + 8 : rows + 16, :] = jnp.ones((8, lanes), F32)
+    for q in range(pairs):
+        pair = (2 * q, 2 * q + 1)
+        for f in pair:
+            loads[f].wait()
+
+        def group(g, _):
+            blocks = []
+            for h in range(2):
+                for slot in range(2):
+                    at = pl.ds(pl.multiple_of(slot * half + h * quarter + g * 8 + 8, 8), 8)
+                    cover = wet[at, :]
+                    block = jnp.zeros((8, lanes), F32)
+                    for f in pair:
+                        for k in range(levels):
+                            place = (2 * h + slot) * width + 2 * ((f - 2 * q) * levels + k)
+                            x = pltpu.roll(padded[f, k, at, :] * cover, place + 1, 1)
+                            block = jnp.where((lane >> 1) == (place >> 1), x, block)
+                    blocks.append(block)
+            to = pl.ds(pl.multiple_of(g * 8, 8), 8)
+            lower = jnp.where(lane < width, blocks[0], blocks[1])
+            upper = jnp.where(lane < 3 * width, blocks[2], blocks[3])
+            lat_pack[q, to, :] = jnp.where(lane < 2 * width, lower, upper)
+            return 0
+
+        lax.fori_loop(0, quarter // 8, group, 0)
+        pl.when(top)(fold[q].start)
+        pl.when(jnp.logical_not(top))(up[q].start)
+        pl.when(lat > 0)(down[q].start)
+
+    first = wet[8:9, :]
+    final = wet[rows + 7 : rows + 8, :]
+    for f in range(fields):
+        at_field = slice(f * levels, (f + 1) * levels)
+        lon_pack[0, at_field, :] = jnp.concatenate([padded[f, k, 8:9, :] for k in range(levels)], 0) * first
+        lon_pack[1, at_field, :] = (
+            jnp.concatenate([padded[f, k, rows + 7 : rows + 8, :] for k in range(levels)], 0) * final
+        )
     east.start()
     west.start()
 
@@ -143,64 +168,78 @@
         branch = jnp.maximum(largest, 1) - 1
     branch_ref[0] = jnp.max(branch)
     east.wait_recv()
-    west_ref[...] = west_in[...]
     west.wait_recv()
-    east_ref[...] = east_in[...]
+    for f in range(fields):
+        for k in range(levels):
+            i = f * levels + k
+            padded[f, k, 7:8, :] = west_in[i : i + 1, :]
+            padded[f, k, rows + 8 : rows + 9, :] = east_in[i : i + 1, :]
 
     @pl.when(lat > 0)
     def _():
-        up.wait_recv()
+        for copy in up:
+            copy.wait_recv()
 
     @pl.when(lat == 0)
     def _():
         south_in[...] = jnp.zeros_like(south_in)
 
-    down.wait_recv()
-    place = lax.broadcasted_iota(jnp.int32, (half, lanes), 1)
-    south = pltpu.roll(south_in[...], 2, 1)
-
-    @pl.when(top)
-    def _():
-        r = lax.broadcasted_iota(jnp.int32, (half, half), 0)
-        c = lax.broadcasted_iota(jnp.int32, (half, half), 1)
-        turn = jnp.where(r + c == half - 1, 1.0, 0.0).astype(F32)
-        mirror = jnp.dot(turn, north_in[...], precision=lax.Precision.HIGHEST, preferred_element_type=F32)
-        mirror = pltpu.roll(mirror, 65, 1)
-        mirror = jnp.where((place & 63) >= 32, -mirror, mirror)
-        lat_ref[...] = jnp.where((place & 1) == 1, mirror, south)
-
-    @pl.when(jnp.logical_not(top))
-    def _():
-        lat_ref[...] = jnp.where((place & 1) == 1, north_in[...], south)
-
-    up.wait_send()
-    pl.when(lat > 0)(down.wait_send)
+    for copy in down:
+        copy.wait_recv()
+    sub = lax.broadcasted_iota(jnp.int32, (8, lanes), 0)
+    odd = (lane & 1) == 1
+    outer = (lane // width) % 2 == 1
+    groups = quarter // 8
+    for q in range(pairs):
+        sign = 1.0 if q == 0 else -1.0
+
+        @pl.when(top)
+        def _():
+            for g in range(groups):
+                x = north_in[q, (groups - 1 - g) * 8 : (groups - g) * 8, :]
+                x = pltpu.roll(x, 4, 0)
+                x = jnp.where((sub & 2) == 0, pltpu.roll(x, 6, 0), pltpu.roll(x, 2, 0))
+                x = jnp.where((sub & 1) == 0, pltpu.roll(x, 7, 0), pltpu.roll(x, 1, 0))
+                x = jnp.where(outer, pltpu.roll(x, 3 * width + 1, 1), pltpu.roll(x, width + 1, 1)) * sign
+                south = pltpu.roll(south_in[q, g * 8 : g * 8 + 8, :], 2, 1)
+                lat_ref[q, g * 8 : g * 8 + 8, :] = jnp.where(odd, x, south)
+
+        @pl.when(jnp.logical_not(top))
+        def _():
+            for g in range(groups):
+                south = pltpu.roll(south_in[q, g * 8 : g * 8 + 8, :], 2, 1)
+                lat_ref[q, g * 8 : g * 8 + 8, :] = jnp.where(odd, north_in[q, g * 8 : g * 8 + 8, :], south)
+
+    diff_load.wait()
+    for q in range(pairs):
+        up[q].wait_send()
+        pl.when(lat > 0)(down[q].wait_send)
     east.wait_send()
     west.wait_send()
     for t in tell:
         t.wait_send()
 
 
-def halos(relays, plan, state, mask):
+def halos(relays, plan, state, mask, diffusivity):
     fields, levels, rows, lanes = state.shape
     bands = lax.axis_size("lat")
-    pack = (rows // 2, lanes)
+    pack = (fields // 2, rows // 4, lanes)
     edge = (fields * levels, lanes)
     near = pl.BlockSpec(memory_space=pltpu.VMEM)
     anywhere = pl.BlockSpec(memory_space=pl.ANY)
     scalars = pl.BlockSpec(memory_space=pltpu.SMEM)
     return pl.pallas_call(
         functools.partial(halo_kernel, relays),
-        in_specs=[scalars, anywhere, anywhere],
-        out_specs=[near, near, near, scalars],
+        in_specs=[scalars, anywhere, anywhere, anywhere],
+        out_specs=[near, near, near, near, scalars],
         out_shape=[
             jax.ShapeDtypeStruct(pack, F32),
-            jax.ShapeDtypeStruct(edge, F32),
-            jax.ShapeDtypeStruct(edge, F32),
+            jax.ShapeDtypeStruct((fields, levels, rows + 16, lanes), F32),
+            jax.ShapeDtypeStruct((rows + 16, lanes), F32),
+            jax.ShapeDtypeStruct(diffusivity.shape, F32),
             jax.ShapeDtypeStruct((1,), jnp.int32),
         ],
         scratch_shapes=[
-            pltpu.VMEM(state.shape, F32),
             pltpu.VMEM(mask.shape, jnp.int32),
             pltpu.VMEM(pack, F32),
             pltpu.VMEM((2,) + edge, F32),
@@ -210,14 +249,14 @@
             pltpu.VMEM(edge, F32),
             pltpu.VMEM((8, lanes), jnp.int32),
             pltpu.VMEM((bands - 1, 8, lanes), jnp.int32),
-            pltpu.SemaphoreType.DMA((fields + 1,)),
-            pltpu.SemaphoreType.DMA((4 + bands - 1,)),
-            pltpu.SemaphoreType.DMA((4 + bands - 1,)),
+            pltpu.SemaphoreType.DMA((fields + 2,)),
+            pltpu.SemaphoreType.DMA((fields + 2 + bands - 1,)),
+            pltpu.SemaphoreType.DMA((fields + 2 + bands - 1,)),
         ],
         compiler_params=pltpu.CompilerParams(
-            collective_id=0, has_side_effects=True, vmem_limit_bytes=16 * MIB
+            collective_id=0, has_side_effects=True, vmem_limit_bytes=55 * MIB
         ),
-    )(plan, state, mask)
+    )(plan, state, mask, diffusivity)
 
 
 def leaves(plan_ref, chips, chip, t, way):
@@ -236,15 +275,11 @@
     rounds,
     idle,
     plan_ref,
-    state_ref,
-    diff_ref,
-    mask_ref,
-    lat_ref,
-    west_ref,
-    east_ref,
-    out_ref,
     padded,
     wet,
+    diff_ref,
+    lat_ref,
+    out_ref,
     mine,
     theirs,
     other,
@@ -253,9 +288,6 @@
     arrived,
     swapped,
     relayed,
-    result,
-    load_sem,
-    store_sem,
     half_send,
     half_recv,
     tile_send,
@@ -267,7 +299,7 @@
     relay_send,
     relay_recv,
 ):
-    fields, levels, rows, lanes = state_ref.shape
+    fields, levels, rows, lanes = out_ref.shape
     planes = fields * levels
     quarter = rows // 4
     chunks = quarter // STEP
@@ -293,10 +325,6 @@
         if idle is not None:
             pl.when(lat == idle)(work)
 
-    loads = [
-        pltpu.make_async_copy(state_ref.at[f], padded.at[f, :, pl.ds(8, rows), :], load_sem.at[f])
-        for f in range(fields)
-    ]
     barrier = pltpu.get_barrier_semaphore()
 
     def greet(who):
@@ -317,18 +345,6 @@
         for o in range(1, bands):
             for at in (lon, ahead_lon, behind_lon):
                 greet({"lat": (idle + o) % bands, "lon": at})
-
-    for load in loads:
-        load.start()
-
-    wet[pl.ds(8, rows), :] = mask_ref[...].astype(F32)
-    wet[0:8, :] = jnp.ones((8, lanes), F32)
-    wet[rows + 8 : rows + 16, :] = jnp.ones((8, lanes), F32)
-    for f in range(fields):
-        for k in range(levels):
-            i = f * levels + k
-            padded[f, k, 7:8, :] = west_ref[i : i + 1, :]
-            padded[f, k, rows + 8 : rows + 9, :] = east_ref[i : i + 1, :]
 
     chosen = {}
     for side, (way, _) in enumerate(ways):
@@ -349,7 +365,9 @@
         def group(slot, _):
             row = pl.multiple_of(half * quarter + c * STEP, STEP)
             base = pl.multiple_of(slot * (2 * quarter) + row, STEP)
-            edges = pltpu.roll(lat_ref[pl.ds(row, STEP), :], 64 * slot, 1)
+            turn = lax.rem(lanes - (2 * half + slot) * (lanes // 4), lanes)
+            at = pl.ds(pl.multiple_of(c * STEP, STEP), STEP)
+            edges = [pltpu.roll(lat_ref[q, at, :], turn, 1) for q in range(fields // 2)]
             wet_c = wet[pl.ds(base + 8, STEP), :]
             wet_e = wet[pl.ds(base + 9, STEP), :]
             wet_w = wet[pl.ds(base + 7, STEP), :]
@@ -361,10 +379,9 @@
                 u, v = center[2], center[3]
                 grad_x, grad_y, value = [], [], []
                 for f in range(fields):
-                    i = f * levels + k
                     e = padded[f, k, pl.ds(base + 9, STEP), :] * wet_e
                     w = padded[f, k, pl.ds(base + 7, STEP), :] * wet_w
-                    edge = pltpu.roll(edges, (lanes - 2 - 2 * i) % lanes, 1)
+                    edge = pltpu.roll(edges[f // 2], lanes - 2 - 2 * (f % 2 * levels + k), 1)
                     n = jnp.where(is_last, edge, pltpu.roll(center[f], lanes - 1, 1))
                     s = jnp.where(is_first, edge, pltpu.roll(center[f], 1, 1))
                     gx, gy = e - w, n - s
@@ -430,7 +447,7 @@
         )
 
     relay_chunks = chunks // 2
-    relays = RELAYED * relay_chunks - 1
+    relays = min(RELAYS, RELAYED * relay_chunks)
 
     def part_of(n):
         return n // RELAYED, pl.ds(lax.rem(n, RELAYED) * levels, levels)
@@ -483,11 +500,10 @@
         if idle is None:
             work(slice(0, planes))
             return
-        pl.when(c < relay_chunks - 1)(lambda: work(pl.ds(RELAYED * levels, planes - RELAYED * levels)))
-        pl.when(c == relay_chunks - 1)(
-            lambda: work(pl.ds((RELAYED - 1) * levels, planes - (RELAYED - 1) * levels))
-        )
-        pl.when(c >= relay_chunks)(lambda: work(slice(0, planes)))
+        for number in range(RELAYED + 1):
+            skipped = number * levels
+            around = jnp.clip(relays - c * RELAYED, 0, RELAYED) == number
+            pl.when(around)(functools.partial(work, pl.ds(skipped, planes - skipped)))
 
     def each_relay(c, work):
         if idle is None:
@@ -496,9 +512,6 @@
             n = c * RELAYED + f
             pl.when(n < relays)(functools.partial(work, n))
 
-    for load in loads:
-        load.wait()
-
     def advance(c, _):
         solve(c, 1 - core, theirs)
 
@@ -539,7 +552,7 @@
 
         @resting
         def _():
-            @pl.when(c > 0)
+            @pl.when((c > 0) & (c - 1 < (bands - 1) * relays))
             def _():
                 pass_on(c - 1)
 
@@ -565,13 +578,6 @@
             at = jnp.where(came, 4 + side * rounds + jnp.minimum(rank, rounds - 1), at)
         origin.append(at)
 
-    def store(c, slot, part):
-        half = core if part == 0 else 1 - core
-        row = pl.multiple_of(2 * quarter * slot + half * quarter + c * STEP, STEP)
-        return pltpu.make_async_copy(
-            result.at[c, slot, part], out_ref.at[:, :, pl.ds(row, STEP), :], store_sem.at[c, slot, part]
-        )
-
     def place(c):
         second(c).wait_recv()
         resting(first(c).wait_recv)
@@ -590,20 +596,38 @@
                     )
                     values = [ref[c, slot, i] for ref in (near, far) for slot in range(2)]
                     values += [came[side, r, c, i] for side, r in keys]
+                    half = core if part == 0 else 1 - core
                     for slot in range(2):
-                        result[c, slot, part, f, k] = pick(origin[slot], values)
+                        row = pl.multiple_of(2 * quarter * slot + half * quarter + c * STEP, STEP)
+                        out_ref[f, k, pl.ds(row, STEP), :] = pick(origin[slot], values)
             return 0
 
         lax.fori_loop(0, levels, level, 0)
-        for slot in range(2):
-            for part in range(2):
-                store(c, slot, part).start()
 
     def chunk_at(step):
         if idle is None:
             return step
         return step // 2 + relay_chunks * lax.rem(step, 2)
 
+    def finish(c):
+        first(c).wait_send()
+        second(c).wait_send()
+
+        @busy
+        def _():
+            def sent(part):
+                for key in keys:
+                    direct(c, *key, part).wait_send()
+
+            def sent_relay(n):
+                for side in range(2):
+                    detour(side, n).wait_send()
+
+            each_part(c, sent)
+            each_relay(c, sent_relay)
+            for key in keys:
+                swap(c, *key).wait_send()
+
     left = (bands - 1) * relays - (chunks - 1)
     each_step = -(-left // chunks)
 
@@ -636,36 +660,11 @@
         @pl.when(step > 0)
         def _():
             place(chunk_at(step - 1))
+            finish(chunk_at(step - 1))
 
         return 0
 
     lax.fori_loop(0, chunks + 1, drain, 0)
-
-    def finish(c, _):
-        first(c).wait_send()
-        second(c).wait_send()
-
-        @busy
-        def _():
-            def sent(part):
-                for key in keys:
-                    direct(c, *key, part).wait_send()
-
-            def sent_relay(n):
-                for side in range(2):
-                    detour(side, n).wait_send()
-
-            each_part(c, sent)
-            each_relay(c, sent_relay)
-            for key in keys:
-                swap(c, *key).wait_send()
-
-        for slot in range(2):
-            for part in range(2):
-                store(c, slot, part).wait()
-        return 0
-
-    lax.fori_loop(0, chunks, finish, 0)
 
     @resting
     def _():
@@ -678,14 +677,14 @@
         lax.fori_loop(0, relays, relay_sent, 0)
 
 
-def move(rounds, idle, plan, state, diffusivity, mask, lat_edges, west, east):
-    fields, levels, rows, lanes = state.shape
+def move(rounds, idle, plan, padded, wet, diffusivity, lat_edges):
+    fields, levels, rows, lanes = padded.shape
+    rows = rows - 16
     bands = lax.axis_size("lat")
     chunks = rows // 4 // STEP
     planes = fields * levels
-    relays = RELAYED * (chunks // 2) - 1 if idle is not None else 1
+    relays = min(RELAYS, RELAYED * (chunks // 2)) if idle is not None else 1
     others = bands - 1 if idle is not None else 1
-    anywhere = pl.BlockSpec(memory_space=pl.ANY)
     near = pl.BlockSpec(memory_space=pltpu.VMEM)
     halves = pltpu.VMEM((chunks, 2, planes, STEP, lanes), F32)
     pieces = pltpu.VMEM((2, rounds, chunks, planes, STEP, lanes), F32)
@@ -693,12 +692,10 @@
     number = rounds if idle is None else 4 + idle
     return pl.pallas_call(
         functools.partial(move_kernel, rounds, idle),
-        in_specs=[pl.BlockSpec(memory_space=pltpu.SMEM), anywhere] + [near] * 5,
-        out_specs=anywhere,
-        out_shape=jax.ShapeDtypeStruct(state.shape, F32),
+        in_specs=[pl.BlockSpec(memory_space=pltpu.SMEM), near, near, near, near],
+        out_specs=near,
+        out_shape=jax.ShapeDtypeStruct((fields, levels, rows, lanes), F32),
         scratch_shapes=[
-            pltpu.VMEM((fields, levels, rows + 16, lanes), F32),
-            pltpu.VMEM((rows + 16, lanes), F32),
             halves,
             halves,
             halves,
@@ -707,9 +704,6 @@
             pieces,
             pieces,
             pltpu.VMEM((others, 2, relays, levels, STEP, lanes), F32),
-            pltpu.VMEM((chunks, 2, 2, fields, levels, STEP, lanes), F32),
-            dma((fields,)),
-            dma((chunks, 2, 2)),
             dma((chunks, 2)),
             dma((chunks, 2)),
             dma((chunks, 2, rounds)),
@@ -724,16 +718,16 @@
         compiler_params=pltpu.CompilerParams(
             collective_id=number, has_side_effects=True, vmem_limit_bytes=(24 + 6 * rounds) * MIB
         ),
-    )(plan, state, diffusivity, mask, lat_edges, west, east)
+    )(plan, padded, wet, diffusivity, lat_edges)
 
 
 def local(relays, state, diffusivity, mask, tile_plan):
     plan = tile_plan.reshape(-1)
-    lat_edges, west, east, branch = halos(relays, plan, state, mask)
+    lat_edges, padded, wet, diff, branch = halos(relays, plan, state, mask, diffusivity)
     branches = [functools.partial(move, rounds, None) for rounds in (1, 2, 3)]
     if relays:
         branches = [functools.partial(move, 1, row) for row in range(lax.axis_size("lat"))] + branches
-    return lax.switch(branch[0], branches, plan, state, diffusivity, mask, lat_edges, west, east)
+    return lax.switch(branch[0], branches, plan, padded, wet, diff, lat_edges)
 
 
 def solution(mesh):

time: 63.1 us -> 59.9 us (0.949)
  Pallas kernels: 60.2 us -> 57.4 us
    pallas_call x1, Pallas kernels: 47.4 us -> 45.6 us  [move(): pl.pallas_call(functools.partial(move_kernel, rounds, idle), in_specs=[pl...]
    pallas_call x1, Pallas kernels: 12.8 us -> 11.8 us  [halos(): pl.pallas_call(functools.partial(halo_kernel, relays), in_specs=[scalars,...]
    unnamed x7 -> x3, local copies, waits for them, and re-layouts: 2.03 us -> 2.02 us
where the time goes in v2:
time: 59.9 us; the launch traced here: 60.1 us
  Pallas kernels  57.4 us (96%)
  local copies, waits for them, and re-layouts  2.02 us (3%)
  between operations  0.65 us (1%)
    pallas_call x1, Pallas kernels, move(): pl.pallas_call(functools.partial(move_kernel, rounds, idle), in_specs=[pl...  45.6 us
    pallas_call x1, Pallas kernels, halos(): pl.pallas_call(functools.partial(halo_kernel, relays), in_specs=[scalars,...  11.8 us
    unnamed x3, local copies, waits for them, and re-layouts  2.02 us

profile of v2, /device:TPU:1, one launch (start us, length us, event | category | flops | bytes accessed | tf_op | source)
XLA Modules:
  0.0 60.1 jit_solution(5287201799684470376)
XLA Ops:
  0.0 0.0 copy-start
  0.0 11.8 %shard_map.53 = (f32[2,64,128]{2,1,0:T(8,128)S(1)}, f32[4,8,272,128]{3,2,1,0:T(8,128)S(1)}, f32[272,128]{1,0:T(8,128)S(1)}, f32[7,256,128]{2,1,0:T(8,128)S(1)}, s32[1]{0:T(128)}) custom-call(s32[16]{0:T(128)} %bitcast.2, f32[4,8,256,128]{3,2,1,0:T(8,128)} %state_ref.1, s32[256,128]{1,0:T(8,128)} %mask_ref.1, f32[7,256,128]{2,1,0:T(8,128)} %diff_ref.1), custom_call_target="tpu_custom_call" | custom-call | tf_op jit(solution)/shard_map/pallas_call | solution.py:231
  12.4 0.0 copy-done
  12.4 45.6 %conditional.1 = (f32[4,8,256,128]{3,2,1,0:T(8,128)S(1)}) conditional(s32[]{:T(128)} %bitcast.1, (s32[16]{0:T(128)S(1)}, f32[4,8,272,128]{3,2,1,0:T(8,128)S(1)}, f32[272,128]{1,0:T(8,128)S(1)}, f32[7,256,128]{2,1,0:T(8,128)S(1)}, f32[2,64,128]{2,1,0:T(8,128)S(1)}) %tuple.41, (s32[16]{0:T(128)S(1)}, ...), branch_computations={%region_0.0_spmd, %region_1.0_spmd, %region_2.0_spmd, %region_3.0_... | conditional | bytes 8 | solution.py:730
  12.5 45.6 %branch_3_fun.1 = f32[4,8,256,128]{3,2,1,0:T(8,128)S(1)} custom-call(s32[16]{0:T(128)S(1)} %get-tuple-element.98.plan_ref, f32[4,8,272,128]{3,2,1,0:T(8,128)S(1)} %get-tuple-element.99.padded, f32[272,128]{1,0:T(8,128)S(1)} %get-tuple-element.100.wet, f32[7,256,128]{2,1,0:T(8,128)S(1)} %get-tuple-element.101.diff_ref, ...), custom_call_target="tpu_custom_call" | custom-call | tf_op jit(solution)/shard_map/cond/branch_3_fun/pallas_call | solution.py:693
  58.1 2.0 %copy.20 = f32[4,8,256,128]{3,2,1,0:T(8,128)} copy(f32[4,8,256,128]{3,2,1,0:T(8,128)S(1)} %get-tuple-element.128) | data formatting | bytes 8388608
Async XLA Ops:
  0.0 12.4 %copy-start = (s32[16,1]{0,1:T(1,128)S(1)}, s32[16,1]{0,1:T(1,128)}, u32[]{:S(2)}) copy-start(s32[16,1]{0,1:T(1,128)} %param.14) | copy-start | bytes 196

commit v3 on v2

--- a/solution.py
+++ b/solution.py
@@ -18,8 +18,26 @@
 MIB = 1 << 20
 MESH = pl.DeviceIdType.MESH
 STEP = 8
-RELAYS = 7
 RELAYED = 2
+
+
+def relay_plan(idle, bands):
+    busy = [row for row in range(bands) if row not in idle]
+    if len(idle) == 1:
+        row = idle[0]
+        above, below = list(range(bands - 1, row, -1)), list(range(row))
+        groups = []
+        while above or below:
+            groups.append([side.pop(0) for side in (above, below) if side])
+        return {row: groups}, 7
+    if idle[1] < busy[0] or busy[1] < idle[0]:
+        return {idle[0]: [[busy[1]]], idle[1]: [[busy[0]]]}, 10
+    return {idle[0]: [[busy[0]]], idle[1]: [[busy[1]]]}, 14
+
+
+def idle_sets(bands):
+    single = [(row,) for row in range(bands)]
+    return single + [(a, b) for a in range(bands) for b in range(a + 1, bands)]
 
 
 def remote_copy(source, target, send, recv, who):
@@ -158,14 +176,22 @@
         t.wait_recv()
         values.append(counts_in[o])
         value_rows.append(lax.rem(lat + bands - o - 1, bands))
-    largest, idle = values[0], jnp.full(count.shape, bands, jnp.int32)
-    for value, row in zip(values, value_rows):
+    largest = values[0]
+    for value in values[1:]:
         largest = jnp.maximum(largest, value)
-        idle = jnp.minimum(idle, jnp.where(value == 0, row, bands))
+    branch = jnp.maximum(largest, 1) - 1
     if relays:
-        branch = jnp.where(largest <= 1, idle, bands - 1 + largest)
-    else:
-        branch = jnp.maximum(largest, 1) - 1
+        sets = idle_sets(bands)
+        branch = branch + len(sets)
+        rests = []
+        for row in range(bands):
+            at_rest = jnp.zeros(count.shape, jnp.int32)
+            for value, value_row in zip(values, value_rows):
+                at_rest = jnp.where((value == 0) & (value_row == row), 1, at_rest)
+            rests.append(at_rest == 1)
+        for number, rows_at_rest in enumerate(sets):
+            all_rest = functools.reduce(jnp.logical_and, [rests[row] for row in rows_at_rest])
+            branch = jnp.where(all_rest & (largest <= 1), number, branch)
     branch_ref[0] = jnp.max(branch)
     east.wait_recv()
     west.wait_recv()
@@ -313,7 +339,25 @@
     behind_lon = lax.rem(lon + devices - 2, devices)
     ways = ((1, ahead_lon), (-1, behind_lon))
     keys = [(side, r) for side in range(2) for r in range(rounds)]
-    active = None if idle is None else lat != idle
+    if idle is None:
+        served, relays, active, resting_now = {}, 0, None, None
+    else:
+        served, relays = relay_plan(idle, bands)
+        resting_now = functools.reduce(jnp.logical_or, [lat == row for row in idle])
+        active = jnp.logical_not(resting_now)
+        order = {row: sum(groups, []) for row, groups in served.items()}
+        others = len(order[idle[0]])
+        relay_row, relay_at = jnp.int32(0), jnp.int32(0)
+        for row, rows_served in order.items():
+            for j, busy_row in enumerate(rows_served):
+                relay_row = jnp.where(lat == busy_row, row, relay_row)
+                relay_at = jnp.where(lat == busy_row, j, relay_at)
+
+    def served_row(j):
+        row = jnp.int32(0)
+        for at, rows_served in order.items():
+            row = jnp.where(lat == at, pick(j, rows_served), row)
+        return row
 
     def busy(work):
         if idle is None:
@@ -323,7 +367,7 @@
 
     def resting(work):
         if idle is not None:
-            pl.when(lat == idle)(work)
+            pl.when(resting_now)(work)
 
     barrier = pltpu.get_barrier_semaphore()
 
@@ -338,13 +382,13 @@
         greet({"lon": behind_lon})
         if idle is not None:
             for at in (lon, ahead_lon, behind_lon):
-                greet({"lat": idle, "lon": at})
+                greet({"lat": relay_row, "lon": at})
 
     @resting
     def _():
-        for o in range(1, bands):
+        for j in range(others):
             for at in (lon, ahead_lon, behind_lon):
-                greet({"lat": (idle + o) % bands, "lon": at})
+                greet({"lat": served_row(j), "lon": at})
 
     chosen = {}
     for side, (way, _) in enumerate(ways):
@@ -446,21 +490,19 @@
             twin,
         )
 
-    relay_chunks = chunks // 2
-    relays = min(RELAYS, RELAYED * relay_chunks)
 
     def part_of(n):
         return n // RELAYED, pl.ds(lax.rem(n, RELAYED) * levels, levels)
 
     def detour(side, n):
-        j = lax.rem(lat - (idle + 1) + 2 * bands, bands)
+        j = relay_at
         c, part = part_of(n)
         return remote_copy(
             leaving.at[side, 0, c, part],
             relayed.at[j, side, n],
             leg_send.at[side, n],
             leg_recv.at[j, side, n],
-            {"lat": idle, "lon": ways[side][1]},
+            {"lat": relay_row, "lon": ways[side][1]},
         )
 
     def forward(j, side, n):
@@ -470,23 +512,18 @@
             arrived.at[side, 0, c, part],
             relay_send.at[j, side, n],
             relay_recv.at[side, n],
-            {"lat": lax.rem(idle + 1 + j, bands)},
+            {"lat": served_row(j)},
         )
 
     def pass_on(t):
-        groups = []
-        if idle is not None:
-            above, below = list(range(bands - 1, idle, -1)), list(range(idle))
-            while above or below:
-                groups.append([rows.pop(0) for rows in (above, below) if rows])
+        groups = [len(group) for group in served[idle[0]]]
         before, j, n = 0, jnp.int32(0), jnp.int32(0)
-        for group in groups:
-            at = t - before
-            inside = at >= 0
-            which = [(row - idle - 1) % bands for row in group]
-            j = jnp.where(inside, pick(lax.rem(jnp.maximum(at, 0), len(group)), which), j)
-            n = jnp.where(inside, jnp.maximum(at, 0) // len(group), n)
-            before += relays * len(group)
+        for number, size in enumerate(groups):
+            at = jnp.maximum(t - before * relays, 0)
+            inside = t >= before * relays
+            j = jnp.where(inside, before + lax.rem(at, size), j)
+            n = jnp.where(inside, at // size, n)
+            before += size
         for side in range(2):
             here(j, side, n).wait_recv()
             forward(j, side, n).start()
@@ -521,7 +558,7 @@
                 pl.semaphore_wait(barrier, 3)
             else:
                 busy(lambda: pl.semaphore_wait(barrier, 6))
-                resting(lambda: pl.semaphore_wait(barrier, 1 + 3 * (bands - 1)))
+                resting(lambda: pl.semaphore_wait(barrier, 1 + 3 * others))
 
         first(c).start()
         solve(c, core, mine)
@@ -552,7 +589,7 @@
 
         @resting
         def _():
-            @pl.when((c > 0) & (c - 1 < (bands - 1) * relays))
+            @pl.when((c > 0) & (c - 1 < others * relays))
             def _():
                 pass_on(c - 1)
 
@@ -607,7 +644,13 @@
     def chunk_at(step):
         if idle is None:
             return step
-        return step // 2 + relay_chunks * lax.rem(step, 2)
+        arrival, sent = [], 0
+        for c in range(chunks):
+            around = min(max(relays - c * RELAYED, 0), RELAYED)
+            sent += fields - around
+            arrival.append([sent, (c * RELAYED + around) if around else 0])
+        arrival = [max(here / sent, there / relays) for here, there in arrival]
+        return pick(step, sorted(range(chunks), key=lambda c: arrival[c]))
 
     def finish(c):
         first(c).wait_send()
@@ -628,7 +671,7 @@
             for key in keys:
                 swap(c, *key).wait_send()
 
-    left = (bands - 1) * relays - (chunks - 1)
+    left = others * relays - (chunks - 1) if idle is not None else 0
     each_step = -(-left // chunks)
 
     def drain(step, _):
@@ -670,7 +713,7 @@
     def _():
         def relay_sent(n, _):
             for side in range(2):
-                for j in range(bands - 1):
+                for j in range(others):
                     forward(j, side, n).wait_send()
             return 0
 
@@ -683,13 +726,15 @@
     bands = lax.axis_size("lat")
     chunks = rows // 4 // STEP
     planes = fields * levels
-    relays = min(RELAYS, RELAYED * (chunks // 2)) if idle is not None else 1
-    others = bands - 1 if idle is not None else 1
+    others, relays = 1, 1
+    if idle is not None:
+        served, relays = relay_plan(idle, bands)
+        others = sum(len(group) for group in served[idle[0]])
     near = pl.BlockSpec(memory_space=pltpu.VMEM)
     halves = pltpu.VMEM((chunks, 2, planes, STEP, lanes), F32)
     pieces = pltpu.VMEM((2, rounds, chunks, planes, STEP, lanes), F32)
     dma = pltpu.SemaphoreType.DMA
-    number = rounds if idle is None else 4 + idle
+    number = rounds if idle is None else 4 + idle_sets(bands).index(idle)
     return pl.pallas_call(
         functools.partial(move_kernel, rounds, idle),
         in_specs=[pl.BlockSpec(memory_space=pltpu.SMEM), near, near, near, near],
@@ -726,7 +771,7 @@
     lat_edges, padded, wet, diff, branch = halos(relays, plan, state, mask, diffusivity)
     branches = [functools.partial(move, rounds, None) for rounds in (1, 2, 3)]
     if relays:
-        branches = [functools.partial(move, 1, row) for row in range(lax.axis_size("lat"))] + branches
+        branches = [functools.partial(move, 1, idle) for idle in idle_sets(lax.axis_size("lat"))] + branches
     return lax.switch(branch[0], branches, plan, padded, wet, diff, lat_edges)
 
 

time: 59.9 us -> 58.6 us (0.978)
  the two profiles are of different devices: /device:TPU:1 before, /device:TPU:9 now
where the time goes in v3:
time: 58.6 us; the launch traced here: 58.4 us
  Pallas kernels  55.5 us (95%)
  local copies, waits for them, and re-layouts  2.02 us (3%)
  between operations  0.65 us (1%)
    pallas_call x1, Pallas kernels, move(): pl.pallas_call(functools.partial(move_kernel, rounds, idle), in_specs=[pl...  45.4 us
    pallas_call x1, Pallas kernels, halos(): pl.pallas_call(functools.partial(halo_kernel, relays), in_specs=[scalars,...  10.1 us
    unnamed x3, local copies, waits for them, and re-layouts  2.02 us

profile of v3, /device:TPU:9, one launch (start us, length us, event | category | flops | bytes accessed | tf_op | source)
XLA Modules:
  0.0 58.4 jit_solution(1734139665149870880)
XLA Ops:
  0.0 0.0 copy-start
  0.0 10.1 %shard_map.59 = (f32[2,64,128]{2,1,0:T(8,128)S(1)}, f32[4,8,272,128]{3,2,1,0:T(8,128)S(1)}, f32[272,128]{1,0:T(8,128)S(1)}, f32[7,256,128]{2,1,0:T(8,128)S(1)}, s32[1]{0:T(128)}) custom-call(s32[16]{0:T(128)} %bitcast.2, f32[4,8,256,128]{3,2,1,0:T(8,128)} %state_ref.1, s32[256,128]{1,0:T(8,128)} %mask_ref.1, f32[7,256,128]{2,1,0:T(8,128)} %diff_ref.1), custom_call_target="tpu_custom_call" | custom-call | tf_op jit(solution)/shard_map/pallas_call | solution.py:257
  10.8 0.0 copy-done
  10.8 45.6 %conditional.1 = (f32[4,8,256,128]{3,2,1,0:T(8,128)S(1)}) conditional(s32[]{:T(128)} %bitcast.1, (s32[16]{0:T(128)S(1)}, f32[4,8,272,128]{3,2,1,0:T(8,128)S(1)}, f32[272,128]{1,0:T(8,128)S(1)}, f32[7,256,128]{2,1,0:T(8,128)S(1)}, f32[2,64,128]{2,1,0:T(8,128)S(1)}) %tuple.71, (s32[16]{0:T(128)S(1)}, ...), branch_computations={%region_0.0_spmd, %region_1.0_spmd, %region_2.0_spmd, %region_3.0_... | conditional | bytes 8 | solution.py:775
  10.8 45.4 %branch_0_fun.1 = f32[4,8,256,128]{3,2,1,0:T(8,128)S(1)} custom-call(s32[16]{0:T(128)S(1)} %get-tuple-element.135.plan_ref, f32[4,8,272,128]{3,2,1,0:T(8,128)S(1)} %get-tuple-element.136.padded, f32[272,128]{1,0:T(8,128)S(1)} %get-tuple-element.137.wet, f32[7,256,128]{2,1,0:T(8,128)S(1)} %get-tuple-element.144.diff_ref, ...), custom_call_target="tpu_custom_call" | custom-call | tf_op jit(solution)/shard_map/cond/branch_0_fun/pallas_call | solution.py:738
  56.4 2.0 %copy.32 = f32[4,8,256,128]{3,2,1,0:T(8,128)} copy(f32[4,8,256,128]{3,2,1,0:T(8,128)S(1)} %get-tuple-element.224) | data formatting | bytes 8388608
Async XLA Ops:
  0.0 10.8 %copy-start = (s32[16,1]{0,1:T(1,128)S(1)}, s32[16,1]{0,1:T(1,128)}, u32[]{:S(2)}) copy-start(s32[16,1]{0,1:T(1,128)} %param.20) | copy-start | bytes 196
